TPU v7x, 256 devices: a whole 4x4x8 slice. The times are simulated.
256 devices in a mesh: section: 2 (over z_hi), dp: 4 (over x), expert: 32 (over y, z_lo, core).
Axes of the slice: x: 4, y: 4, z: 8 (z_hi: 2, z_lo: 4; z = z_hi * 4 + z_lo), core: 2. Of those that a mesh axis runs over, the one named last changes fastest.
Arguments:
- activations: bfloat16 [2, 16384, 4096], P('section', ('dp', 'expert')), may hold values from -6 to 6
- norm_gain: float32 [2, 4096], P('section'), may hold values from 0.25 to 1.75
- route_ids: int32 [2, 16384, 2], P('section', ('dp', 'expert')), may hold values from 0 to 15, all different within a row; in each aligned block of 128 rows (0 to 127, 128 to 255, ..., all dimensions but the last counted through in order) at most 18 rows name the same one
- route_gates: float32 [2, 16384, 2], P('section', ('dp', 'expert')), may hold values from 0.2 to 1
- gate_weight: bfloat16 [2, 4096, 12288], P('section', None, 'expert'), may hold values from -0.09375 to 0.09375
- up_weight: bfloat16 [2, 4096, 12288], P('section', None, 'expert'), may hold values from -0.09375 to 0.09375
- leak_rates: float32 [2, 12288], P('section', 'expert'), may hold values from 0.2 to 0.9
- down_weight: bfloat16 [2, 12288, 4096], P('section', 'expert', 'dp'), may hold values from -0.21875 to 0.21875
- cotangent: bfloat16 [2, 16384, 4096], P('section', ('dp', 'expert')), may hold values from -6 to 6
Outputs:
- passed_on: bfloat16 [2, 16384, 4096], P('section', ('dp', 'expert'))
- passed_back: bfloat16 [2, 16384, 4096], P('section', ('dp', 'expert'))
- up_grad: bfloat16 [2, 4096, 12288], P('section', 'dp', 'expert')
Inputs may be any that keep to these rules, and one draw needn't show every extreme that they name: `route_ids`: within one section, the 128 tokens of one device name each expert at most 18 times, and some device reaches 18 for some expert; the two experts of a token differ.
All inputs are finite; a program needn't handle non-finite values.
Results may differ from a plain program's by a relative error of at most 0.015.
Values may be sent and summed in bfloat16 or wider, within the bound.
A program may use at most 192 MiB of HBM per device.

v0:
```python
import jax
import jax.numpy as jnp
from jax import lax
from jax.sharding import PartitionSpec as P

TSTEPS = 4
EPS = 1e-06
THETA = 0.5
SHARP = 4.0


def passed_along(value, axis, steps):
    count = lax.axis_size(axis)
    leading, last = (max(0, -steps), min(count, count - steps))
    return lax.ppermute(value, axis, [(source, source + steps) for source in range(leading, last)])


def lif_rate(gate_act, up_act, leak_rate):
    drive = jax.nn.silu(gate_act) * up_act
    volts = jnp.zeros_like(drive)
    spike_sum = jnp.zeros_like(drive)
    for timestep in range(TSTEPS):
        volts = leak_rate * volts + drive
        spikes = jax.nn.sigmoid(SHARP * (volts - THETA)) - jax.nn.sigmoid(SHARP * (-volts - THETA))
        volts = volts - THETA * spikes
        spike_sum = spike_sum + spikes
    return spike_sum / TSTEPS


def to_experts(slot_rows):
    model_width = slot_rows.shape[2]
    doubled = jnp.repeat(slot_rows, 2, axis=0)
    gathered = lax.all_to_all(doubled, "expert", split_axis=0, concat_axis=0, tiled=True)
    return gathered.reshape(-1, model_width)


def from_experts(partials, experts, capacity):
    model_width = partials.shape[2]
    returned = lax.all_to_all(
        partials.astype(jnp.bfloat16), "expert", split_axis=0, concat_axis=0, tiled=True
    ).astype(partials.dtype)
    paired = returned.reshape(experts, 2, capacity, model_width)
    summed = jnp.sum(paired, axis=1).astype(jnp.bfloat16)
    return summed.reshape(experts * capacity, model_width).astype(jnp.float32)


def per_device(
    activations,
    norm_gain,
    route_ids,
    route_gates,
    gate_weight,
    up_weight,
    leak_rates,
    down_weight,
    cotangent,
):
    tok_count = activations.shape[1]
    model_width = activations.shape[2]
    experts = lax.axis_size("expert") // 2
    capacity = min(tok_count, 2 * (9 * tok_count // (8 * experts)))
    tokens = activations[0].astype(jnp.float32)
    gain_row = norm_gain[0]
    inv_rms = lax.rsqrt(jnp.mean(tokens * tokens, axis=-1, keepdims=True) + EPS)
    normed = (tokens * inv_rms * gain_row).astype(jnp.bfloat16)
    flat_ids = route_ids[0].reshape(-1)
    onehot = (flat_ids[:, None] == jnp.arange(experts, dtype=jnp.int32)[None, :]).astype(jnp.int32)
    slot_index = jnp.sum(onehot * (jnp.cumsum(onehot, axis=0) - 1), axis=1)
    places = (flat_ids * capacity + slot_index).reshape(tok_count, 2)
    positions = jnp.arange(experts * capacity, dtype=jnp.int32)[:, None]
    pick_first = positions == places[None, :, 0]
    pick_second = positions == places[None, :, 1]
    pick_both = jnp.logical_or(pick_first, pick_second)
    slot_rows = jnp.dot(
        pick_both.astype(jnp.bfloat16), normed, preferred_element_type=jnp.float32
    ).astype(jnp.bfloat16)
    arrived = to_experts(slot_rows.reshape(experts, capacity, model_width))
    gate_local = gate_weight[0]
    up_local = up_weight[0]
    leak_local = leak_rates[0]
    down_full = lax.all_gather(down_weight[0], "dp", axis=1, tiled=True)
    gate_act = jnp.dot(arrived, gate_local, preferred_element_type=jnp.float32)
    up_act = jnp.dot(arrived, up_local, preferred_element_type=jnp.float32)
    spike_rate = lif_rate(gate_act, up_act, leak_local).astype(jnp.bfloat16)
    out_part = jnp.dot(spike_rate, down_full, preferred_element_type=jnp.float32)
    expert_out = from_experts(out_part.reshape(-1, capacity, model_width), experts, capacity)
    weights = route_gates[0]
    mixing = jnp.where(pick_first.T, weights[:, 0:1], 0.0) + jnp.where(
        pick_second.T, weights[:, 1:2], 0.0
    )
    moe_sum = jnp.dot(
        mixing, expert_out, precision=lax.Precision.HIGHEST, preferred_element_type=jnp.float32
    )
    section_out = (tokens + moe_sum).astype(jnp.bfloat16)
    passed_on = passed_along(section_out[None], "section", 1)
    upstream = cotangent[0].astype(jnp.float32)
    grad_first = (weights[:, 0:1] * upstream).astype(jnp.bfloat16)
    grad_second = (weights[:, 1:2] * upstream).astype(jnp.bfloat16)
    grad_slots = jnp.dot(
        pick_first.astype(jnp.bfloat16), grad_first, preferred_element_type=jnp.float32
    )
    grad_slots = grad_slots + jnp.dot(
        pick_second.astype(jnp.bfloat16), grad_second, preferred_element_type=jnp.float32
    )
    grad_rows = to_experts(grad_slots.astype(jnp.bfloat16).reshape(experts, capacity, model_width))
    rate_grad = lax.dot_general(
        grad_rows, down_full, (((1,), (1,)), ((), ())), preferred_element_type=jnp.float32
    )
    unused_rate, pullback = jax.vjp(
        lambda gate_in, up_in: lif_rate(gate_in, up_in, leak_local), gate_act, up_act
    )
    gate_grad, up_act_grad = pullback(rate_grad)
    gate_grad = gate_grad.astype(jnp.bfloat16)
    up_act_grad = up_act_grad.astype(jnp.bfloat16)
    back_part = lax.dot_general(
        gate_grad, gate_local, (((1,), (1,)), ((), ())), preferred_element_type=jnp.float32
    )
    back_part = back_part + lax.dot_general(
        up_act_grad, up_local, (((1,), (1,)), ((), ())), preferred_element_type=jnp.float32
    )
    route_back = from_experts(back_part.reshape(-1, capacity, model_width), experts, capacity)
    norm_grad = (
        jnp.dot(
            pick_both.T.astype(jnp.float32),
            route_back,
            precision=lax.Precision.HIGHEST,
            preferred_element_type=jnp.float32,
        )
        * gain_row
    )
    section_back = (
        upstream
        + inv_rms * norm_grad
        - tokens
        * (inv_rms * inv_rms * inv_rms)
        * jnp.mean(tokens * norm_grad, axis=-1, keepdims=True)
    )
    passed_back = passed_along(section_back.astype(jnp.bfloat16)[None], "section", -1)
    up_term = lax.dot_general(
        arrived, up_act_grad, (((0,), (0,)), ((), ())), preferred_element_type=jnp.float32
    )
    up_term = up_term.astype(jnp.bfloat16).astype(jnp.float32)
    up_grad = lax.psum_scatter(up_term.astype(jnp.bfloat16), "dp", scatter_dimension=0, tiled=True)[
        None
    ]
    return (passed_on, passed_back, up_grad)


def solution(mesh):
    return jax.shard_map(
        per_device,
        mesh=mesh,
        in_specs=(
            P("section", ("dp", "expert"), None),
            P("section", None),
            P("section", ("dp", "expert"), None),
            P("section", ("dp", "expert"), None),
            P("section", None, "expert"),
            P("section", None, "expert"),
            P("section", "expert"),
            P("section", "expert", "dp"),
            P("section", ("dp", "expert"), None),
        ),
        out_specs=(
            P("section", ("dp", "expert"), None),
            P("section", ("dp", "expert"), None),
            P("section", "dp", "expert"),
        ),
        check_vma=False,
    )
```

profile of v0, /device:TPU:73, one launch (start us, length us, event | category | flops | bytes accessed | tf_op | source)
XLA Modules:
  0.0 713.4 jit_solution(17626897167263078738)
XLA Ops:
  11.2 3.5 convolution_convert_fusion.2
  14.7 4.3 reshape.95
  19.0 5.3 broadcast_in_dim.46
  24.4 8.7 %all-to-all-start = ((bf16[32,18,4096]{2,1,0:T(8,128)(2,1)}), bf16[32,18,4096]{2,1,0:T(8,128)(2,1)}, u32[]{:S(2)}, u32[]{:S(2)}) async-start(bf16[32,18,4096]{2,1,0:T(8,128)(2,1)} %bitcast.85), calls=%async_computation | async-start | bytes 12582912 | tf_op jit(solution)/shard_map/all_to_all | solution.py:33
  37.6 4.3 reshape.100
  42.0 127.4 %all-to-all-done = bf16[32,18,4096]{2,1,0:T(8,128)(2,1)} async-done(((bf16[32,18,4096]{2,1,0:T(8,128)(2,1)}), bf16[32,18,4096]{2,1,0:T(8,128)(2,1)}, u32[]{:S(2)}, u32[]{:S(2)}) %all-to-all-start) | async-done | bytes 4718624 | tf_op jit(solution)/shard_map/all_to_all | solution.py:33
  169.4 5.3 broadcast_in_dim.48
  174.6 9.1 %all-to-all-start.2 = ((bf16[32,18,4096]{2,1,0:T(8,128)(2,1)}), bf16[32,18,4096]{2,1,0:T(8,128)(2,1)}, u32[]{:S(2)}, u32[]{:S(2)}) async-start(bf16[32,18,4096]{2,1,0:T(8,128)(2,1)} %bitcast.84), calls=%async_computation.2 | async-start | bytes 12582912 | tf_op jit(solution)/shard_map/all_to_all | solution.py:33
  184.5 7.7 %reshape.97 = bf16[576,4096]{1,0:T(8,128)(2,1)} reshape(bf16[32,18,4096]{2,1,0:T(8,128)(2,1)} %all-to-all-done) | data formatting | bytes 9437184 | tf_op jit(solution)/shard_map/reshape | solution.py:34
  192.2 7.0 fusion.7
  199.2 3.5 fusion.11
  202.7 25.7 %all-gather.3.cloned.1.call-done = bf16[1,384,4096]{2,1,0:T(8,128)(2,1)} async-done(((bf16[1,384,1024]{2,1,0:T(8,128)(2,1)}), bf16[1,384,4096]{2,1,0:T(8,128)(2,1)}) %all-gather.3.cloned.1.call-update) | async-done | bytes 3145744 | tf_op jit(solution)/shard_map/all_gather | solution.py:81
  228.5 9.4 %convolution_convert_fusion = bf16[576,4096]{1,0:T(8,128)(2,1)} fusion(bf16[1,384,4096]{2,1,0:T(8,128)(2,1)} %all-gather.3.cloned.1.call-done, f32[384]{0:T(512)S(1)} %reduce.5, f32[384]{0:T(512)S(1)} %broadcast_multiply_fusion, f32[576,384]{1,0:T(8,128)} %fusion.7, f32[576,384]{1,0:T(8,128)} %fusion.11), kind=kOutput, calls=%fused_computation.3 | convolution fusion | flops 1830002688 | bytes 9636864 | tf_op jit(solution)/shard_map/dot_general | solution.py:85
  237.9 7.6 %convert_element_type.93 = bf16[32,18,4096]{2,1,0:T(8,128)(2,1)} reshape(bf16[576,4096]{1,0:T(8,128)(2,1)} %convolution_convert_fusion) | data formatting | bytes 9437184 | tf_op jit(solution)/shard_map/convert_element_type | solution.py:40
  245.5 74.4 %all-to-all-done.2 = bf16[32,18,4096]{2,1,0:T(8,128)(2,1)} async-done(((bf16[32,18,4096]{2,1,0:T(8,128)(2,1)}), bf16[32,18,4096]{2,1,0:T(8,128)(2,1)}, u32[]{:S(2)}, u32[]{:S(2)}) %all-to-all-start.2) | async-done | bytes 4718624 | tf_op jit(solution)/shard_map/all_to_all | solution.py:33
  320.0 9.7 %all-to-all-start.1 = ((bf16[32,18,4096]{2,1,0:T(8,128)(2,1)}), bf16[32,18,4096]{2,1,0:T(8,128)(2,1)}, u32[]{:S(2)}, u32[]{:S(2)}) async-start(bf16[32,18,4096]{2,1,0:T(8,128)(2,1)} %convert_element_type.93), calls=%async_computation.1 | async-start | bytes 12582912 | tf_op jit(solution)/shard_map/all_to_all | solution.py:39
  329.7 7.7 %reshape.102 = bf16[576,4096]{1,0:T(8,128)(2,1)} reshape(bf16[32,18,4096]{2,1,0:T(8,128)(2,1)} %all-to-all-done.2) | data formatting | bytes 9437184 | tf_op jit(solution)/shard_map/reshape | solution.py:34
  337.4 10.1 %multiply_convert_fusion = (bf16[576,384]{1,0:T(8,128)(2,1)S(1)}, f32[576,384]{1,0:T(8,128)S(1)}) fusion(f32[576,384]{1,0:T(8,128)} %fusion.11, f32[576,384]{1,0:T(8,128)} %fusion.7, f32[384]{0:T(512)S(1)} %broadcast_multiply_fusion, f32[384]{0:T(512)S(1)} %reduce.5, bf16[576,4096]{1,0:T(8,128)(2,1)} %reshape.102, ...), kind=kOutput, calls=%fused_computation.87 | convolution fusion | flops 1840693248 | bytes 10963968 | tf_op jit(solution)/shard_map/dot_general | solution.py:106
  350.3 4.3 add_convert_fusion
  354.6 7.6 %convert_element_type.105 = bf16[32,18,4096]{2,1,0:T(8,128)(2,1)} reshape(bf16[576,4096]{1,0:T(8,128)(2,1)} %add_convert_fusion) | data formatting | bytes 9437184 | tf_op jit(solution)/shard_map/convert_element_type | solution.py:40
  362.3 103.5 %all-to-all-done.1 = bf16[32,18,4096]{2,1,0:T(8,128)(2,1)} async-done(((bf16[32,18,4096]{2,1,0:T(8,128)(2,1)}), bf16[32,18,4096]{2,1,0:T(8,128)(2,1)}, u32[]{:S(2)}, u32[]{:S(2)}) %all-to-all-start.1) | async-done | bytes 4718624 | tf_op jit(solution)/shard_map/all_to_all | solution.py:39
  465.7 9.0 %all-to-all-start.3 = ((bf16[32,18,4096]{2,1,0:T(8,128)(2,1)}), bf16[32,18,4096]{2,1,0:T(8,128)(2,1)}, u32[]{:S(2)}, u32[]{:S(2)}) async-start(bf16[32,18,4096]{2,1,0:T(8,128)(2,1)} %convert_element_type.105), calls=%async_computation.3 | async-start | bytes 12582912 | tf_op jit(solution)/shard_map/all_to_all | solution.py:39
  475.0 7.3 %convolution_convert_fusion.1 = bf16[4096,384]{1,0:T(8,128)(2,1)} fusion(bf16[576,4096]{1,0:T(8,128)(2,1)} %reshape.97, bf16[576,384]{1,0:T(8,128)(2,1)} %copy-done.8), kind=kOutput, calls=%fused_computation.4 | convolution fusion | flops 1813512192 | bytes 8306688 | tf_op jit(solution)/shard_map/dot_general | solution.py:139
  482.4 6.8 bitcast_reduce_fusion.1
  489.2 4.3 convert_element_type.95
  493.5 5.3 fusion.2
  498.8 7.0 collective-permute-start
  505.8 127.6 %all-to-all-done.3 = bf16[32,18,4096]{2,1,0:T(8,128)(2,1)} async-done(((bf16[32,18,4096]{2,1,0:T(8,128)(2,1)}), bf16[32,18,4096]{2,1,0:T(8,128)(2,1)}, u32[]{:S(2)}, u32[]{:S(2)}) %all-to-all-start.3) | async-done | bytes 4718624 | tf_op jit(solution)/shard_map/all_to_all | solution.py:39
  633.5 6.9 bitcast_reduce_fusion
  640.3 4.3 convert_element_type.107
  644.7 2.9 fusion.21
  649.8 52.0 %collective-permute-done.1 = bf16[1,128,4096]{2,1,0:T(8,128)(2,1)} collective-permute-done((bf16[1,128,4096]{2,1,0:T(8,128)(2,1)S(1)}, bf16[1,128,4096]{2,1,0:T(8,128)(2,1)}, u32[]{:S(2)}, u32[]{:S(2)}) %collective-permute-start.1) | collective-permute-done | bytes 1048608 | tf_op jit(solution)/shard_map/ppermute | solution.py:15
  (55 shorter events, 18.9 us)
Async XLA Ops:
  7.2 192.0 %copy-start = (bf16[1,4096,384]{2,1,0:T(8,128)(2,1)S(1)}, bf16[1,4096,384]{2,1,0:T(8,128)(2,1)}, u32[]{:S(2)}) copy-start(bf16[1,4096,384]{2,1,0:T(8,128)(2,1)} %param.13) | copy-start | bytes 9437188
  24.4 8.7 %copy-start.11 = (f32[1,128,2]{1,2,0:T(2,128)S(1)}, f32[1,128,2]{1,2,0:T(2,128)}, u32[]{:S(2)}) copy-start(f32[1,128,2]{1,2,0:T(2,128)} %param.12) | copy-start | bytes 3076
  24.4 145.0 %all-to-all-start = ((bf16[32,18,4096]{2,1,0:T(8,128)(2,1)}), bf16[32,18,4096]{2,1,0:T(8,128)(2,1)}, u32[]{:S(2)}, u32[]{:S(2)}) async-start(bf16[32,18,4096]{2,1,0:T(8,128)(2,1)} %bitcast.85), calls=%async_computation | async-start | bytes 12582912 | tf_op jit(solution)/shard_map/all_to_all | solution.py:33
  33.1 2.2 copy-start.2
  174.6 9.8 %copy-start.10 = (f32[1,384]{1,0:T(1,128)S(1)}, f32[1,384]{1,0:T(1,128)}, u32[]{:S(2)}) copy-start(f32[1,384]{1,0:T(1,128)} %param.15) | copy-start | bytes 4612
  174.6 145.3 %all-to-all-start.2 = ((bf16[32,18,4096]{2,1,0:T(8,128)(2,1)}), bf16[32,18,4096]{2,1,0:T(8,128)(2,1)}, u32[]{:S(2)}, u32[]{:S(2)}) async-start(bf16[32,18,4096]{2,1,0:T(8,128)(2,1)} %bitcast.84), calls=%async_computation.2 | async-start | bytes 12582912 | tf_op jit(solution)/shard_map/all_to_all | solution.py:33
  183.7 44.7 %all-gather.3.cloned.1.call-start = ((), (), s32[]{:S(2)}) async-start(), calls=%async_computation.6 | async-start | bytes 3932160 | tf_op jit(solution)/shard_map/all_gather | solution.py:81
  192.2 7.0 copy-start.4
  320.0 145.8 %all-to-all-start.1 = ((bf16[32,18,4096]{2,1,0:T(8,128)(2,1)}), bf16[32,18,4096]{2,1,0:T(8,128)(2,1)}, u32[]{:S(2)}, u32[]{:S(2)}) async-start(bf16[32,18,4096]{2,1,0:T(8,128)(2,1)} %convert_element_type.93), calls=%async_computation.1 | async-start | bytes 12582912 | tf_op jit(solution)/shard_map/all_to_all | solution.py:39
  337.4 10.1 %copy-start.6 = (f32[576,384]{1,0:T(8,128)S(1)}, f32[576,384]{1,0:T(8,128)}, u32[]{:S(2)}) copy-start(f32[576,384]{1,0:T(8,128)} %fusion.7) | copy-start | bytes 2654212
  337.4 10.2 %copy-start.7 = (f32[576,384]{1,0:T(8,128)S(1)}, f32[576,384]{1,0:T(8,128)}, u32[]{:S(2)}) copy-start(f32[576,384]{1,0:T(8,128)} %fusion.11) | copy-start | bytes 2654212
  347.6 2.8 copy-start.8
  347.6 2.7 copy-start.5
  465.7 167.7 %all-to-all-start.3 = ((bf16[32,18,4096]{2,1,0:T(8,128)(2,1)}), bf16[32,18,4096]{2,1,0:T(8,128)(2,1)}, u32[]{:S(2)}, u32[]{:S(2)}) async-start(bf16[32,18,4096]{2,1,0:T(8,128)(2,1)} %convert_element_type.105), calls=%async_computation.3 | async-start | bytes 12582912 | tf_op jit(solution)/shard_map/all_to_all | solution.py:39
  474.8 227.0 %reduce-scatter.2.cloned.1.call-start = ((), (), s32[]{:S(2)}) async-start(), calls=%async_computation.5 | async-start | bytes 3932160 | tf_op jit(solution)/shard_map/reduce_scatter | solution.py:143
  498.8 151.0 %collective-permute-start = (bf16[1,128,4096]{2,1,0:T(8,128)(2,1)}, bf16[1,128,4096]{2,1,0:T(8,128)(2,1)}, u32[]{:S(2)}, u32[]{:S(2)}) collective-permute-start(bf16[1,128,4096]{2,1,0:T(8,128)(2,1)} %fusion.2), channel_id=1, source_target_pairs={{0,128},{1,129},{2,130},{3,131},{4,132},{5,133},{6,134},{7,135},{8... | collective-permute-start | bytes 3145736 | tf_op jit(solution)/shard_map/ppermute | solution.py:15
  640.3 4.3 copy-start.9
  644.7 3.0 copy-start.1
  644.7 3.0 copy-start.3
  648.5 53.3 %collective-permute-start.1 = (bf16[1,128,4096]{2,1,0:T(8,128)(2,1)S(1)}, bf16[1,128,4096]{2,1,0:T(8,128)(2,1)}, u32[]{:S(2)}, u32[]{:S(2)}) collective-permute-start(bf16[1,128,4096]{2,1,0:T(8,128)(2,1)S(1)} %fusion.26), channel_id=1, source_target_pairs={{128,0},{129,1},{130,2},{131,3},{132,4},{133,5},{134,6},{135,7},{1... | collective-permute-start | bytes 3145736 | tf_op jit(solution)/shard_map/ppermute | solution.py:15
Sparse Core Ops, SparseCore 0:
  186.4 42.0 all-gather.2
  482.5 40.8 reduce-scatter.1
where the time goes:
time: 720 us; the launch traced here: 713 us
  waiting for transfers between devices  511 us (71%)
  local copies, waits for them, and re-layouts  65 us (9%)
  matrix products  60.6 us (8%)
  starting transfers between devices  45.4 us (6%)
  other arithmetic  16.8 us (2%)
  between operations  14.5 us (2%)
    all_to_all x2, waiting for transfers between devices, from_experts(): lax.all_to_all(partials.astype(jnp.bfloat16), 'expert', split_axis=0, con...  231 us
    all_to_all x2, waiting for transfers between devices, to_experts(): lax.all_to_all(doubled, 'expert', split_axis=0, concat_axis=0, tiled=True)  202 us
    ppermute x2, waiting for transfers between devices, passed_along(): lax.ppermute(value, axis, [(source, source + steps) for source in range(l...  52 us
    all_gather x1, waiting for transfers between devices, per_device(): down_full = lax.all_gather(down_weight[0], 'dp', axis=1, tiled=True)  25.7 us
    all_to_all x2, starting transfers between devices, from_experts(): lax.all_to_all(partials.astype(jnp.bfloat16), 'expert', split_axis=0, con...  18.7 us
    all_to_all x2, starting transfers between devices, to_experts(): lax.all_to_all(doubled, 'expert', split_axis=0, concat_axis=0, tiled=True)  17.8 us
    reshape x2, local copies, waits for them, and re-layouts, to_experts(): return gathered.reshape(-1, model_width)  15.5 us
    convert_element_type x2, local copies, waits for them, and re-layouts, from_experts(): partials.astype(jnp.bfloat16)  15.2 us
  transfers between devices with their start and end apart: 8, of which 6 were waited for; matrix products, arithmetic and copies ran while one was open for 16% of the time, Pallas kernels for 0%

commit v1 on v0

--- a/solution.py
+++ b/solution.py
@@ -78,7 +78,9 @@
     gate_local = gate_weight[0]
     up_local = up_weight[0]
     leak_local = leak_rates[0]
-    down_full = lax.all_gather(down_weight[0], "dp", axis=1, tiled=True)
+    down_full = jnp.concatenate(
+        lax.all_to_all(jnp.stack([down_weight[0]] * lax.axis_size("dp")), "dp", 0, 0), axis=1
+    )
     gate_act = jnp.dot(arrived, gate_local, preferred_element_type=jnp.float32)
     up_act = jnp.dot(arrived, up_local, preferred_element_type=jnp.float32)
     spike_rate = lif_rate(gate_act, up_act, leak_local).astype(jnp.bfloat16)

time: 720 us -> 782 us (1.086)
  waiting for transfers between devices: 511 us -> 562 us
  local copies, waits for them, and re-layouts: 65 us -> 77 us
    all_to_all x2, waiting for transfers between devices: 202 us -> 241 us  [to_experts(): lax.all_to_all(doubled, 'expert', split_axis=0, concat_axis=0, tiled=True)]
    all_to_all x0 -> x1, waiting for transfers between devices: none -> 26 us  [per_device(): lax.all_to_all(jnp.stack([down_weight[0]] * lax.axis_size('dp')), 'dp', 0...]
    all_gather x1 -> x0, waiting for transfers between devices: 25.7 us -> none  [per_device(): down_full = lax.all_gather(down_weight[0], 'dp', axis=1, tiled=True)]
    all_to_all x2, waiting for transfers between devices: 231 us -> 250 us  [from_experts(): lax.all_to_all(partials.astype(jnp.bfloat16), 'expert', split_axis=0, con...]
    reshape x0 -> x3, local copies, waits for them, and re-layouts: none -> 12.3 us  [per_device(): jnp.concatenate(lax.all_to_all(jnp.stack([down_weight[0]] * lax.axis_size...]
  transfers between devices with their start and end apart: 8 -> 8, of which waited for: 6 -> 6; matrix products, arithmetic and copies ran while one was open for 16% -> 12% of each run, Pallas kernels for 0% -> 0%
where the time goes in v1:
time: 782 us; the launch traced here: 774 us
  waiting for transfers between devices  562 us (72%)
  local copies, waits for them, and re-layouts  77 us (10%)
  matrix products  54.4 us (7%)
  starting transfers between devices  51.1 us (7%)
  other arithmetic  15.5 us (2%)
  between operations  14.5 us (2%)
    all_to_all x2, waiting for transfers between devices, from_experts(): lax.all_to_all(partials.astype(jnp.bfloat16), 'expert', split_axis=0, con...  250 us
    all_to_all x2, waiting for transfers between devices, to_experts(): lax.all_to_all(doubled, 'expert', split_axis=0, concat_axis=0, tiled=True)  241 us
    ppermute x2, waiting for transfers between devices, passed_along(): lax.ppermute(value, axis, [(source, source + steps) for source in range(l...  44.2 us
    all_to_all x1, waiting for transfers between devices, per_device(): lax.all_to_all(jnp.stack([down_weight[0]] * lax.axis_size('dp')), 'dp', 0...  26 us
    all_to_all x2, starting transfers between devices, to_experts(): lax.all_to_all(doubled, 'expert', split_axis=0, concat_axis=0, tiled=True)  19.3 us
    all_to_all x2, starting transfers between devices, from_experts(): lax.all_to_all(partials.astype(jnp.bfloat16), 'expert', split_axis=0, con...  18.4 us
  transfers between devices with their start and end apart: 8, of which 6 were waited for; matrix products, arithmetic and copies ran while one was open for 12% of the time, Pallas kernels for 0%

profile of v1, /device:TPU:73, one launch (start us, length us, event | category | flops | bytes accessed | tf_op | source)
XLA Modules:
  0.0 774.2 jit_solution(9300133928581210448)
XLA Ops:
  10.5 4.8 all-to-all-start.1
  22.1 4.3 reshape.102
  26.4 26.0 %all-to-all-done.1 = bf16[4,384,1024]{2,1,0:T(8,128)(2,1)} async-done(((bf16[4,384,1024]{2,1,0:T(8,128)(2,1)}), bf16[4,384,1024]{2,1,0:T(8,128)(2,1)}, u32[]{:S(2)}, u32[]{:S(2)}) %all-to-all-start.1) | async-done | bytes 3145760 | tf_op jit(solution)/shard_map/all_to_all | solution.py:82
  52.4 5.3 broadcast_in_dim.46
  57.7 9.6 %all-to-all-start = ((bf16[32,18,4096]{2,1,0:T(8,128)(2,1)}), bf16[32,18,4096]{2,1,0:T(8,128)(2,1)}, u32[]{:S(2)}, u32[]{:S(2)}) async-start(bf16[32,18,4096]{2,1,0:T(8,128)(2,1)} %bitcast.79), calls=%async_computation | async-start | bytes 12582912 | tf_op jit(solution)/shard_map/all_to_all | solution.py:33
  71.9 4.3 reshape.109
  76.2 127.4 %all-to-all-done = bf16[32,18,4096]{2,1,0:T(8,128)(2,1)} async-done(((bf16[32,18,4096]{2,1,0:T(8,128)(2,1)}), bf16[32,18,4096]{2,1,0:T(8,128)(2,1)}, u32[]{:S(2)}, u32[]{:S(2)}) %all-to-all-start) | async-done | bytes 4718624 | tf_op jit(solution)/shard_map/all_to_all | solution.py:33
  203.6 5.3 broadcast_in_dim.48
  208.9 9.7 %all-to-all-start.3 = ((bf16[32,18,4096]{2,1,0:T(8,128)(2,1)}), bf16[32,18,4096]{2,1,0:T(8,128)(2,1)}, u32[]{:S(2)}, u32[]{:S(2)}) async-start(bf16[32,18,4096]{2,1,0:T(8,128)(2,1)} %bitcast.80), calls=%async_computation.3 | async-start | bytes 12582912 | tf_op jit(solution)/shard_map/all_to_all | solution.py:33
  218.6 4.0 copy.34
  222.6 7.7 reshape.104
  230.4 7.0 fusion.4
  240.9 113.8 %all-to-all-done.3 = bf16[32,18,4096]{2,1,0:T(8,128)(2,1)} async-done(((bf16[32,18,4096]{2,1,0:T(8,128)(2,1)}), bf16[32,18,4096]{2,1,0:T(8,128)(2,1)}, u32[]{:S(2)}, u32[]{:S(2)}) %all-to-all-start.3) | async-done | bytes 4718624 | tf_op jit(solution)/shard_map/all_to_all | solution.py:33
  354.6 7.7 reshape.111
  362.4 10.3 %multiply_convert_fusion = (bf16[576,384]{1,0:T(8,128)(2,1)S(1)}, bf16[576,384]{1,0:T(8,128)(2,1)}, f32[576,384]{1,0:T(8,128)S(1)}) fusion(f32[576,384]{1,0:T(8,128)} %fusion.8, f32[384]{0:T(512)S(1)} %reduce.5, f32[576,384]{1,0:T(8,128)} %fusion.4, f32[384]{0:T(512)S(1)} %broadcast_multiply_fusion, bf16[576,4096]{1,0:T(8,128)(2,1)} %reshape.111, ...), kind=kOutput, calls=%fused_computation.84 | convolution fusion | flops 1842020352 | bytes 11406336 | tf_op jit(solution)/shard_map/dot_general | solution.py:108
  375.5 4.3 add_convert_fusion
  379.8 7.6 convert_element_type.101
  387.4 9.4 %all-to-all-start.4 = ((bf16[32,18,4096]{2,1,0:T(8,128)(2,1)}), bf16[32,18,4096]{2,1,0:T(8,128)(2,1)}, u32[]{:S(2)}, u32[]{:S(2)}) async-start(bf16[32,18,4096]{2,1,0:T(8,128)(2,1)} %convert_element_type.101), calls=%async_computation.4 | async-start | bytes 12582912 | tf_op jit(solution)/shard_map/all_to_all | solution.py:39
  396.8 4.3 copy.27
  401.1 4.0 reshape.116
  406.3 4.7 convolution_convert_fusion
  411.0 5.4 copy.29
  416.4 116.5 %all-to-all-done.4 = bf16[32,18,4096]{2,1,0:T(8,128)(2,1)} async-done(((bf16[32,18,4096]{2,1,0:T(8,128)(2,1)}), bf16[32,18,4096]{2,1,0:T(8,128)(2,1)}, u32[]{:S(2)}, u32[]{:S(2)}) %all-to-all-start.4) | async-done | bytes 4718624 | tf_op jit(solution)/shard_map/all_to_all | solution.py:39
  532.8 9.0 %all-to-all-start.2 = ((bf16[32,18,4096]{2,1,0:T(8,128)(2,1)}), bf16[32,18,4096]{2,1,0:T(8,128)(2,1)}, u32[]{:S(2)}, u32[]{:S(2)}) async-start(bf16[32,18,4096]{2,1,0:T(8,128)(2,1)} %copy.29), calls=%async_computation.2 | async-start | bytes 12582912 | tf_op jit(solution)/shard_map/all_to_all | solution.py:39
  542.1 7.3 convolution_convert_fusion.1
  549.4 6.9 bitcast_reduce_fusion
  556.3 4.6 convert_element_type.103
  566.7 133.9 %all-to-all-done.2 = bf16[32,18,4096]{2,1,0:T(8,128)(2,1)} async-done(((bf16[32,18,4096]{2,1,0:T(8,128)(2,1)}), bf16[32,18,4096]{2,1,0:T(8,128)(2,1)}, u32[]{:S(2)}, u32[]{:S(2)}) %all-to-all-start.2) | async-done | bytes 4718624 | tf_op jit(solution)/shard_map/all_to_all | solution.py:39
  700.6 4.4 bitcast_reduce_fusion.1
  707.3 3.9 fusion.2
  711.2 7.1 collective-permute-start
  718.3 44.2 %collective-permute-done = bf16[1,128,4096]{2,1,0:T(8,128)(2,1)} collective-permute-done((bf16[1,128,4096]{2,1,0:T(8,128)(2,1)S(1)}, bf16[1,128,4096]{2,1,0:T(8,128)(2,1)}, u32[]{:S(2)}, u32[]{:S(2)}) %collective-permute-start) | collective-permute-done | bytes 1048608 | tf_op jit(solution)/shard_map/ppermute | solution.py:15
  (65 shorter events, 34.8 us)
Async XLA Ops:
  7.2 230.2 %copy-start = (bf16[1,4096,384]{2,1,0:T(8,128)(2,1)S(1)}, bf16[1,4096,384]{2,1,0:T(8,128)(2,1)}, u32[]{:S(2)}) copy-start(bf16[1,4096,384]{2,1,0:T(8,128)(2,1)} %param.13) | copy-start | bytes 9437188
  10.5 4.8 copy-start.13
  10.5 8.0 %copy-start.11 = (f32[1,4096]{1,0:T(1,128)S(1)}, f32[1,4096]{1,0:T(1,128)}, u32[]{:S(2)}) copy-start(f32[1,4096]{1,0:T(1,128)} %param.10) | copy-start | bytes 49156
  10.5 41.8 %all-to-all-start.1 = ((bf16[4,384,1024]{2,1,0:T(8,128)(2,1)}), bf16[4,384,1024]{2,1,0:T(8,128)(2,1)}, u32[]{:S(2)}, u32[]{:S(2)}) async-start(bf16[4,384,1024]{2,1,0:T(8,128)(2,1)} %stack.3), calls=%async_computation.1 | async-start | bytes 6291456 | tf_op jit(solution)/shard_map/all_to_all | solution.py:82
  57.7 9.6 %copy-start.14 = (f32[1,128,2]{1,2,0:T(2,128)S(1)}, f32[1,128,2]{1,2,0:T(2,128)}, u32[]{:S(2)}) copy-start(f32[1,128,2]{1,2,0:T(2,128)} %param.12) | copy-start | bytes 3076
  57.7 145.9 %all-to-all-start = ((bf16[32,18,4096]{2,1,0:T(8,128)(2,1)}), bf16[32,18,4096]{2,1,0:T(8,128)(2,1)}, u32[]{:S(2)}, u32[]{:S(2)}) async-start(bf16[32,18,4096]{2,1,0:T(8,128)(2,1)} %bitcast.79), calls=%async_computation | async-start | bytes 12582912 | tf_op jit(solution)/shard_map/all_to_all | solution.py:33
  67.3 2.2 copy-start.3
  208.9 9.7 %copy-start.12 = (f32[1,384]{1,0:T(1,128)S(1)}, f32[1,384]{1,0:T(1,128)}, u32[]{:S(2)}) copy-start(f32[1,384]{1,0:T(1,128)} %param.15) | copy-start | bytes 4612
  208.9 145.8 %all-to-all-start.3 = ((bf16[32,18,4096]{2,1,0:T(8,128)(2,1)}), bf16[32,18,4096]{2,1,0:T(8,128)(2,1)}, u32[]{:S(2)}, u32[]{:S(2)}) async-start(bf16[32,18,4096]{2,1,0:T(8,128)(2,1)} %bitcast.80), calls=%async_computation.3 | async-start | bytes 12582912 | tf_op jit(solution)/shard_map/all_to_all | solution.py:33
  230.4 7.0 copy-start.5
  362.4 10.4 %copy-start.7 = (f32[576,384]{1,0:T(8,128)S(1)}, f32[576,384]{1,0:T(8,128)}, u32[]{:S(2)}) copy-start(f32[576,384]{1,0:T(8,128)} %fusion.4) | copy-start | bytes 2654212
  362.4 10.4 %copy-start.8 = (f32[576,384]{1,0:T(8,128)S(1)}, f32[576,384]{1,0:T(8,128)}, u32[]{:S(2)}) copy-start(f32[576,384]{1,0:T(8,128)} %fusion.8) | copy-start | bytes 2654212
  372.7 2.7 copy-start.9
  372.7 2.7 copy-start.6
  387.4 145.4 %all-to-all-start.4 = ((bf16[32,18,4096]{2,1,0:T(8,128)(2,1)}), bf16[32,18,4096]{2,1,0:T(8,128)(2,1)}, u32[]{:S(2)}, u32[]{:S(2)}) async-start(bf16[32,18,4096]{2,1,0:T(8,128)(2,1)} %convert_element_type.101), calls=%async_computation.4 | async-start | bytes 12582912 | tf_op jit(solution)/shard_map/all_to_all | solution.py:39
  416.4 125.7 %copy-start.10 = (bf16[576,384]{1,0:T(8,128)(2,1)S(1)}, bf16[576,384]{1,0:T(8,128)(2,1)}, u32[]{:S(2)}) copy-start(bf16[576,384]{1,0:T(8,128)(2,1)} %copy-done.9) | copy-start | bytes 1327108
  532.8 167.7 %all-to-all-start.2 = ((bf16[32,18,4096]{2,1,0:T(8,128)(2,1)}), bf16[32,18,4096]{2,1,0:T(8,128)(2,1)}, u32[]{:S(2)}, u32[]{:S(2)}) async-start(bf16[32,18,4096]{2,1,0:T(8,128)(2,1)} %copy.29), calls=%async_computation.2 | async-start | bytes 12582912 | tf_op jit(solution)/shard_map/all_to_all | solution.py:39
  541.9 220.7 %reduce-scatter.2.cloned.1.call-start = ((), (), s32[]{:S(2)}) async-start(), calls=%async_computation.6 | async-start | bytes 3932160 | tf_op jit(solution)/shard_map/reduce_scatter | solution.py:145
  556.3 4.6 copy-start.2
  560.9 2.6 copy-start.4
  565.4 152.9 %collective-permute-start.1 = (bf16[1,128,4096]{2,1,0:T(8,128)(2,1)}, bf16[1,128,4096]{2,1,0:T(8,128)(2,1)}, u32[]{:S(2)}, u32[]{:S(2)}) collective-permute-start(bf16[1,128,4096]{2,1,0:T(8,128)(2,1)} %fusion.20), channel_id=1, source_target_pairs={{128,0},{129,1},{130,2},{131,3},{132,4},{133,5},{134,6},{135,7},{1... | collective-permute-start | bytes 3145736 | tf_op jit(solution)/shard_map/ppermute | solution.py:15
  707.3 59.8 %copy-start.1 = (bf16[1,4096,384]{2,1,0:T(8,128)(2,1)S(1)}, bf16[1,4096,384]{2,1,0:T(8,128)(2,1)}, u32[]{:S(2)}) copy-start(bf16[1,4096,384]{2,1,0:T(8,128)(2,1)} %param.13) | copy-start | bytes 9437188
  711.2 51.3 %collective-permute-start = (bf16[1,128,4096]{2,1,0:T(8,128)(2,1)S(1)}, bf16[1,128,4096]{2,1,0:T(8,128)(2,1)}, u32[]{:S(2)}, u32[]{:S(2)}) collective-permute-start(bf16[1,128,4096]{2,1,0:T(8,128)(2,1)S(1)} %fusion.2), channel_id=1, source_target_pairs={{0,128},{1,129},{2,130},{3,131},{4,132},{5,133},{6,134},{7,135},{8... | collective-permute-start | bytes 3145736 | tf_op jit(solution)/shard_map/ppermute | solution.py:15
Sparse Core Ops, SparseCore 0:
  549.5 38.9 reduce-scatter.1
